TPU v7x, 256 devices: a whole 4x4x8 slice. The times are simulated.
256 devices in a mesh: blk: 64 (over y, z, core), shard: 4 (over x).
Axes of the slice: x: 4, y: 4, z: 8, core: 2. Of those that a mesh axis runs over, the one named last changes fastest.
Arguments:
- gradient: float32 [64, 1024, 1024], P(None, ('shard', 'blk')), may hold values from -55 to 55
- owner_table: int32 [64], replicated, may hold values from 0 to 63, each once
- restart_steps: int32 [64], P('blk'), may hold values from 1 to 9
- left_basis: float32 [64, 1024, 1024], P('blk', 'shard'), may hold values from -0.2 to 1.2, as said below
- right_basis: float32 [64, 1024, 1024], P('blk', 'shard'), may hold values from -0.2 to 1.2, as said below
- first_moment: float32 [64, 1024, 1024], P('blk', 'shard'), may hold values from -3 to 3
- second_moment: float32 [64, 1024, 1024], P('blk', 'shard'), may hold values from 0.016 to 1
Outputs:
- update: float32 [64, 1024, 1024], P(None, ('shard', 'blk'))
- new_first: float32 [64, 1024, 1024], P('blk', 'shard')
- new_second: float32 [64, 1024, 1024], P('blk', 'shard')
Inputs may be any that keep to these rules, and one draw needn't show every extreme that they name: `owner_table`: each block number appears once. `left_basis`: nonsingular, not exactly orthogonal. `right_basis`: nonsingular, not exactly orthogonal.
All inputs are finite; a program needn't handle non-finite values.
Results may differ from a plain program's by a relative error of at most 0.0003.
Values sent between devices are 32-bit elements; how exact they have to be, the bound alone decides.
A program may use at most 64 MiB of HBM per device.

v0:
```python
import functools

import jax
import jax.numpy as jnp
from jax import lax
from jax.experimental import pallas as pl
from jax.experimental.pallas import tpu as pltpu
from jax.sharding import PartitionSpec as P

BETA_ONE = 0.9
BETA_TWO = 0.95
EPSILON = 1e-08
MESH = pl.DeviceIdType.MESH
F32 = jnp.float32
BF16 = jnp.bfloat16
NC = 4
NG = 4
PER = NC // NG
CUTS = ((0, 128), (128, 128), (256, 256), (512, 256), (768, 256))
W = 1024 // NC
Q = 256
NN = (((1,), (0,)), ((), ()))
NT = (((1,), (1,)), ((), ()))

SEMS = {}


def _sems(name, count=1):
    SEMS[name] = (sum(c for _, c in SEMS.values()), count)


for _name in ("L", "R", "M1", "M2", "RS", "RX", "RF", "BI", "RO", "O", "SA", "SB", "GI"):
    _sems(_name)
_sems("G", NG)
for _name in ("A", "C", "X"):
    _sems(_name, NC)
for _name in ("US", "UX", "UF"):
    _sems(_name, len(CUTS))
N_SEMS = sum(c for _, c in SEMS.values())


def split(value):
    high = value.astype(BF16)
    low = (value - high.astype(F32)).astype(BF16)
    return high, low


def dot3(ah, al, bh, bl, dims):
    dot = functools.partial(lax.dot_general, dimension_numbers=dims, preferred_element_type=F32)
    return dot(ah, bh) + (dot(ah, bl) + dot(al, bh))


def kernel(
    owner, steps, grad_in, left_in, right_in, first_in, second_in,
    recv_o, rot_out, graft_out,
    grad, send_g, recv_g, gh, gl, lf, lh, ll, lth, ltl, rf, rh, rl,
    a_snd, a_rcv, b_buf, c_snd, c_rcv, d_buf, x_rcv, rot, m1, m2, dh, dl,
    u0, u1, u2, u3, u4, back, bias_mine, bias, sa_v, sa_r, sb_v, sb_r, norm_g, norm_b, ssem, rsem, bar,
):
    b = lax.axis_index("blk")
    x = lax.axis_index("shard")
    y, z, c = b // 16, (b // 2) % 8, b % 2
    h = x // 2
    xp = x + 1 - 2 * (x % 2)
    home = c == h
    u_all = (u0, u1, u2, u3, u4)
    away = c != h
    q = jnp.where(home, x, 3 - x)
    q_sib = 3 - q
    q_xp = jnp.where(home, xp, 3 - xp)
    q_xps = 3 - q_xp
    slot = (y * 8 + z) * 2 + h

    def dev(xx, yy, zz, cc):
        return {"shard": xx, "blk": (yy * 8 + zz) * 2 + cc}

    sib = dev(x, y, z, 1 - c)
    across = dev(xp, y, z, c)
    swap = dev(3 - x, y, z, 1 - c)

    def sem(ref, name, i=0):
        return ref.at[SEMS[name][0] + i]

    def rcopy(src, dst, name, to, i=0):
        return pltpu.make_async_remote_copy(
            src_ref=src, dst_ref=dst, send_sem=sem(ssem, name, i), recv_sem=sem(rsem, name, i),
            device_id=to, device_id_type=MESH,
        )

    def arrived(ref, name, i=0):
        pltpu.make_async_copy(ref, ref, sem(rsem, name, i)).wait()

    def sent(ref, name, i=0):
        pltpu.make_async_copy(ref, ref, sem(ssem, name, i)).wait()

    def zpeer(i):
        return dev(x, y, (z + i) % 8, c)

    def ypeer(i):
        return dev(x, (y + i) % 4, z, c)

    def xcpeer(i):
        xc = (x * 2 + c + i) % 8
        return dev(xc // 2, y, z, xc % 2)

    gate = pltpu.get_barrier_semaphore()
    for i in range(1, 8):
        pl.semaphore_signal(gate, inc=1, device_id=xcpeer(i), device_id_type=MESH)

    @pl.when(home)
    def _():
        for count, peer in ((8, zpeer), (4, ypeer)):
            for i in range(1, count):
                pl.semaphore_signal(gate, inc=1, device_id=peer(i), device_id_type=MESH)

    grad_copy = pltpu.make_async_copy(grad_in, grad, sem(rsem, "GI"))
    grad_copy.start()
    pl.semaphore_wait(gate, jnp.where(home, 17, 7))

    def fetch(src, dst, name):
        @pl.when(home)
        def _():
            pltpu.make_async_copy(src, dst, sem(rsem, name)).start()

        @pl.when(away)
        def _():
            rcopy(src, dst, name, swap).start()

    fetch(left_in.at[0], lf, "L")

    @pl.when(home)
    def _():
        rcopy(right_in.at[0], rf.at[q], "RX", across).start()
        rcopy(right_in.at[0], rf.at[q], "RS", sib).start()
        pltpu.make_async_copy(right_in.at[0], rf.at[q], sem(rsem, "R")).start()
        for i in range(1, 8):
            pl.semaphore_signal(bar.at[0], inc=1, device_id=zpeer(i), device_id_type=MESH)

    time = jnp.full((8, 128), steps[0].astype(F32))
    row = lax.broadcasted_iota(jnp.int32, (8, 128), 0)
    power = jnp.where(row == 0, jnp.power(jnp.float32(BETA_ONE), time), jnp.power(jnp.float32(BETA_TWO), time))
    bias_mine[...] = 1.0 - power
    rcopy(bias_mine, bias, "BI", sib).start()
    grad_copy.wait()

    @pl.loop(0, 64)
    def _(o):
        rows = grad[owner[o]]
        for k in range(NC):
            send_g[o, k] = rows[:, k * W:(k + 1) * W]

    @pl.when(home)
    def _():
        pl.semaphore_wait(bar.at[0], 7)
        for i in range(1, 4):
            pl.semaphore_signal(bar.at[1], inc=1, device_id=ypeer(i), device_id_type=MESH)
        pl.semaphore_wait(bar.at[1], 3)
        pl.semaphore_signal(bar.at[2], inc=1, device_id=sib, device_id_type=MESH)

    @pl.when(away)
    def _():
        pl.semaphore_wait(bar.at[2], 1)

    for g in range(NG):
        @pl.loop(0, 64)
        def _(t):
            yo, zo, co = (y + t // 16) % 4, (z + (t // 2) % 8) % 8, (c + t) % 2
            o = (yo * 8 + zo) * 2 + co
            xo = jnp.where(co == h, x, 3 - x)
            is_self = jnp.logical_and(home, t == 0)
            src = send_g.at[o, pl.ds((2 * co + g * PER) % NC, PER)]
            dst = recv_g.at[pl.ds(g * PER, PER), b]

            @pl.when(is_self)
            def _():
                pltpu.make_async_copy(src, dst, sem(rsem, "G", g)).start()

            @pl.when(jnp.logical_not(is_self))
            def _():
                rcopy(src, dst, "G", dev(xo, yo, zo, h), g).start()

        @pl.when(away)
        def _():
            part = pl.ds(g * (Q // NG), Q // NG)
            rcopy(right_in.at[0, part], rf.at[x, part], "R", swap).start()

    fetch(first_in.at[0], m1, "M1")
    fetch(second_in.at[0], m2, "M2")

    norm_g[...] = jnp.zeros_like(norm_g)

    @pl.loop(0, 64)
    def _(o):
        mine = grad[o]
        square = mine * mine
        total = square[:, 0:128]
        for k in range(1, 8):
            total = total + square[:, k * 128:(k + 1) * 128]
        norm_g[...] += total

    def split_right(k):
        @pl.loop(0, 4)
        def _(i):
            rows = pl.ds(pl.multiple_of(i * 64, 64), 64)
            high, low = split(rf[k, rows, :])
            rh[k, rows, :] = high
            rl[k, rows, :] = low

    @pl.when(home)
    def _():
        arrived(rf.at[q], "R")
        arrived(rf.at[q_xp], "RX")
        rcopy(rf.at[q_xp], rf.at[q_xp], "RF", sib).start()

    @pl.when(away)
    def _():
        arrived(rf.at[q_sib], "RS")
        arrived(rf.at[q_xps], "RF")

    split_right(2 * h)
    split_right(2 * h + 1)

    arrived(lf, "L")
    for k in range(4):
        cols = slice(k * Q, (k + 1) * Q)
        part = lf[:, cols]
        high, low = split(part)
        lh[:, cols] = high
        ll[:, cols] = low
        high, low = split(part.T)
        lth[k] = high
        ltl[k] = low

    def partial(k, i):
        return dot3(lth[k], ltl[k], gh[i], gl[i], NN)

    for i in range(NC):
        if i % PER == 0:
            arrived(recv_g.at[pl.ds(i, PER)], "G", i // PER)

        @pl.loop(0, 16)
        def _(k):
            rows = pl.ds(pl.multiple_of(k * 16, 16), 16)
            part = jnp.concatenate([recv_g[i, k * 4 + r] for r in range(4)], axis=0)
            high, low = split(part)
            gh[i, rows, :] = high
            gl[i, rows, :] = low

        a_snd[i] = partial(q_xps, i)
        rcopy(a_snd.at[i], a_rcv.at[i], "A", sib, i).start()
        mine = partial(q_xp, i)
        arrived(a_rcv.at[i], "A", i)
        b_buf[i] = mine + a_rcv[i]
        rcopy(b_buf.at[i], x_rcv.at[i], "X", across, i).start()
        c_snd[i] = partial(q_sib, i)
        rcopy(c_snd.at[i], c_rcv.at[i], "C", sib, i).start()
        d_buf[i] = partial(q, i)

    @pl.when(away)
    def _():
        arrived(rf.at[q], "R")
        rcopy(rf.at[q], rf.at[q], "RX", across).start()
        rcopy(rf.at[q], rf.at[q], "RS", sib).start()

    def rotate(i):
        arrived(c_rcv.at[i], "C", i)
        arrived(x_rcv.at[i], "X", i)
        k = (2 * h + i) % 4
        th, tl = split(d_buf[i] + c_rcv[i] + x_rcv[i])
        term = dot3(th, tl, rh[k], rl[k], NN)
        if i == 0:
            rot[...] = term
        else:
            rot[...] += term

    @pl.when(away)
    def _():
        arrived(rf.at[q_xp], "RX")
        rcopy(rf.at[q_xp], rf.at[q_xp], "RF", sib).start()

    @pl.when(home)
    def _():
        arrived(rf.at[q_sib], "RS")
        arrived(rf.at[q_xps], "RF")

    split_right(2 - 2 * h)
    split_right(3 - 2 * h)
    for i in range(NC):
        rotate(i)

    fetch_out = rot_out.at[0]

    @pl.when(home)
    def _():
        pltpu.make_async_copy(rot, fetch_out, sem(rsem, "RO")).start()

    @pl.when(away)
    def _():
        rcopy(rot, fetch_out, "RO", swap).start()

    arrived(bias, "BI")
    arrived(m1, "M1")
    arrived(m2, "M2")
    biases = jnp.where(home, bias_mine[...], bias[...])
    one_over = 1.0 / biases
    scale_one, scale_two = one_over[0:1, 0:1], one_over[1:2, 0:1]

    @pl.loop(0, 8)
    def _(i):
        rows = pl.ds(pl.multiple_of(i * 32, 32), 32)
        value = rot[rows, :]
        first_new = BETA_ONE * m1[rows, :] + (1.0 - BETA_ONE) * value
        second_new = BETA_TWO * m2[rows, :] + (1.0 - BETA_TWO) * value * value
        direction = (first_new * scale_one) / (jnp.sqrt(second_new * scale_two) + EPSILON)
        high, low = split(direction)
        dh[rows, :] = high
        dl[rows, :] = low

    for j, (start, width) in enumerate(CUTS):
        rows = slice(start % Q, start % Q + width)
        u_all[j][q] = dot3(dh[...], dl[...], rh[start // Q, rows, :], rl[start // Q, rows, :], NT)
        mine = u_all[j].at[q]
        rcopy(mine, mine, "UX", across, j).start()
        rcopy(mine, mine, "US", sib, j).start()

    norm_b[...] = jnp.zeros_like(norm_b)
    zc = z * 2 + c
    xy = x * 4 + y
    for j, (start, width) in enumerate(CUTS):
        cols = slice(start, start + width)
        theirs = u_all[j].at[q_xp]
        arrived(theirs, "UX", j)
        rcopy(theirs, theirs, "UF", sib, j).start()
        arrived(u_all[j].at[q_sib], "US", j)
        arrived(u_all[j].at[q_xps], "UF", j)
        uh, ul = split(u_all[j][...].reshape(1024, width))
        result = dot3(lh[...], ll[...], uh, ul, NN)
        square = result * result
        total = square[:, 0:128]
        for k in range(1, width // 128):
            total = total + square[:, k * 128:(k + 1) * 128]
        norm_b[...] += jnp.sum(total.reshape(32, 8, 128), axis=0)

        if j == len(CUTS) - 1:
            sa_v[...] = jnp.concatenate([norm_g[...], norm_b[0:4, :] + norm_b[4:8, :]], axis=0)

            @pl.loop(1, 16)
            def _(i):
                other = (zc + i) % 16
                rcopy(sa_v, sa_r.at[i - 1], "SA", dev(x, y, other // 2, other % 2)).start()

        for i in range(64):
            back[i, :, cols] = result[i * 4:(i + 1) * 4, :]

        @pl.loop(0, 64)
        def _(t):
            yo, zo, co = (y + t // 16) % 4, (z + (t // 2) % 8) % 8, (c + t) % 2
            o = (yo * 8 + zo) * 2 + co
            is_self = jnp.logical_and(home, t == 0)

            @pl.when(is_self)
            def _():
                pltpu.make_async_copy(back.at[o, :, cols], recv_o.at[slot, :, cols], sem(rsem, "O")).start()

            @pl.when(jnp.logical_not(is_self))
            def _():
                rcopy(back.at[o, :, cols], recv_o.at[slot, :, cols], "O", dev(q, yo, zo, co)).start()

    arrived(sa_r, "SA")
    sb_v[...] = sa_v[...] + jnp.sum(sa_r[...], axis=0)

    @pl.loop(1, 16)
    def _(i):
        other = (xy + i) % 16
        rcopy(sb_v, sb_r.at[i - 1], "SB", dev(other // 4, other % 4, z, c)).start()

    arrived(sb_r, "SB")
    totals = sb_v[...] + jnp.sum(sb_r[...], axis=0)
    grad_total = jnp.sum(totals[0:4, :], keepdims=True)
    back_total = jnp.sum(totals[4:8, :], keepdims=True)
    graft = jnp.sqrt(grad_total / back_total)
    graft_out[...] = jnp.broadcast_to(graft, (8, 128))
    arrived(recv_o, "O")
    arrived(rot, "RO")

    sent(sa_r, "SA")
    sent(sb_r, "SB")
    sent(bias, "BI")
    sent(rf.at[0], "RS")
    sent(rf.at[0], "RX")
    sent(rf.at[0], "RF")
    for j in range(NC):
        sent(a_snd.at[j], "A", j)
        sent(b_buf.at[j], "X", j)
        sent(c_snd.at[j], "C", j)
    for j in range(len(CUTS)):
        for name in ("US", "UX", "UF"):
            sent(u_all[j].at[0], name, j)

    @pl.when(home)
    def _():
        for g in range(NG):
            sent(recv_g.at[pl.ds(0, PER), pl.ds(0, 63)], "G", g)
        sent(recv_o.at[pl.ds(0, 63)], "O")

    @pl.when(away)
    def _():
        for g in range(NG):
            sent(recv_g.at[pl.ds(0, PER)], "G", g)
        sent(recv_o, "O")
        sent(lf, "L")
        sent(rf.at[0], "R")
        sent(m1, "M1")
        sent(m2, "M2")
        sent(rot, "RO")


def finish(
    owner, graft, received, rot_in, first_in, second_in, update, first_out, second_out,
    wire, rot, first, second, n1, n2, sin, sout,
):
    parts = 2
    size = Q // parts
    copy = pltpu.make_async_copy

    def pieces(p):
        rows = pl.ds(p * size, size)
        return [
            copy(src.at[0, rows], dst.at[rows], sin.at[p, k])
            for k, (src, dst) in enumerate(((rot_in, rot), (first_in, first), (second_in, second)))
        ]

    def results(p):
        rows = pl.ds(p * size, size)
        return [
            copy(src.at[rows], dst.at[0, rows], sout.at[p, k])
            for k, (src, dst) in enumerate(((n1, first_out), (n2, second_out)))
        ]

    incoming = copy(received, wire, sin.at[parts, 0])
    incoming.start()
    for p in range(parts):
        for piece in pieces(p):
            piece.start()
    scale = graft[0:1, 0:1]
    incoming.wait()

    @pl.loop(0, 64)
    def _(o):
        wire[o] = wire[o] * scale
        copy(wire.at[o], update.at[owner[o]], sout.at[parts, 0]).start()

    for p in range(parts):
        for piece in pieces(p):
            piece.wait()
        rows = pl.ds(p * size, size)
        value = rot[rows, :]
        n1[rows, :] = BETA_ONE * first[rows, :] + (1.0 - BETA_ONE) * value
        n2[rows, :] = BETA_TWO * second[rows, :] + (1.0 - BETA_TWO) * value * value
        for result in results(p):
            result.start()
    for p in range(parts):
        for result in results(p):
            result.wait()
    copy(wire, update, sout.at[parts, 0]).wait()


def body(gradient, owner_table, restart_steps, left_basis, right_basis, first_moment, second_moment):
    vmem = pl.BlockSpec(memory_space=pltpu.VMEM)
    smem = pl.BlockSpec(memory_space=pltpu.SMEM)
    anywhere = pl.BlockSpec(memory_space=pl.ANY)
    rows_f = pltpu.VMEM((Q, 1024), F32)
    rows_b = pltpu.VMEM((Q, 1024), BF16)
    wire = pltpu.VMEM((64, 4, 1024), F32)
    chunks = pltpu.VMEM((NC, Q, W), F32)
    chunks_b = pltpu.VMEM((NC, Q, W), BF16)
    tile = pltpu.VMEM((8, 128), F32)
    lt = pltpu.VMEM((4, Q, Q), BF16)
    whole_b = pltpu.VMEM((4, Q, 1024), BF16)
    fifteen = pltpu.VMEM((15, 8, 128), F32)
    received, rotated, graft = pl.pallas_call(
        kernel,
        out_shape=(
            jax.ShapeDtypeStruct((64, 4, 1024), F32),
            jax.ShapeDtypeStruct((1, Q, 1024), F32),
            jax.ShapeDtypeStruct((8, 128), F32),
        ),
        in_specs=[smem, smem, anywhere, anywhere, anywhere, anywhere, anywhere],
        out_specs=(anywhere, anywhere, vmem),
        scratch_shapes=[
            wire, pltpu.VMEM((64, NC, 4, W), F32), pltpu.VMEM((NC, 64, 4, W), F32),
            chunks_b, chunks_b, rows_f, rows_b, rows_b, lt, lt,
            pltpu.VMEM((4, Q, 1024), F32), whole_b, whole_b,
            chunks, chunks, chunks, chunks, chunks, chunks, chunks,
            rows_f, rows_f, rows_f, rows_b, rows_b,
            *(pltpu.VMEM((4, Q, width), F32) for _, width in CUTS), wire,
            tile, tile, tile, fifteen, tile, fifteen,
            pltpu.VMEM((4, 128), F32), tile,
            pltpu.SemaphoreType.DMA((N_SEMS,)),
            pltpu.SemaphoreType.DMA((N_SEMS,)),
            pltpu.SemaphoreType.REGULAR((3,)),
        ],
        compiler_params=pltpu.CompilerParams(
            collective_id=0, has_side_effects=True, vmem_limit_bytes=56 * 1024 * 1024
        ),
    )(owner_table, restart_steps, gradient, left_basis, right_basis, first_moment, second_moment)

    return pl.pallas_call(
        finish,
        out_shape=(
            jax.ShapeDtypeStruct((64, 4, 1024), F32),
            jax.ShapeDtypeStruct((1, Q, 1024), F32),
            jax.ShapeDtypeStruct((1, Q, 1024), F32),
        ),
        in_specs=[smem, vmem, anywhere, anywhere, anywhere, anywhere],
        out_specs=(anywhere, anywhere, anywhere),
        scratch_shapes=[
            wire, rows_f, rows_f, rows_f, rows_f, rows_f,
            pltpu.SemaphoreType.DMA((3, 3)), pltpu.SemaphoreType.DMA((3, 3)),
        ],
        compiler_params=pltpu.CompilerParams(vmem_limit_bytes=56 * 1024 * 1024),
    )(owner_table, graft, received, rotated, first_moment, second_moment)


def solution(mesh):
    in_specs = (
        P(None, ("shard", "blk"), None),
        P(),
        P("blk"),
        P("blk", "shard", None),
        P("blk", "shard", None),
        P("blk", "shard", None),
        P("blk", "shard", None),
    )
    out_specs = (P(None, ("shard", "blk"), None), P("blk", "shard", None), P("blk", "shard", None))
    return jax.shard_map(body, mesh=mesh, in_specs=in_specs, out_specs=out_specs, check_vma=False)
```

profile of v0, /device:TPU:1, one launch (start us, length us, event | category | flops | bytes accessed | tf_op | source)
XLA Modules:
  0.0 121.8 jit_solution(9044753295685076504)
XLA Ops:
  1.3 114.7 %shard_map.94 = (f32[64,4,1024]{2,1,0:T(4,128)}, f32[1,256,1024]{2,1,0:T(8,128)}, f32[8,128]{1,0:T(8,128)}) custom-call(s32[64]{0:T(128)} %owner.3, s32[1]{0:T(128)S(6)} %copy.10.steps, f32[64,4,1024]{2,1,0:T(4,128)} %grad_in.1, f32[1,256,1024]{2,1,0:T(8,128)} %left_in.1, f32[1,256,1024]{2,1,0:T(8,128)} %right_in.1, f32[1,256,1024]{2,1,0:T(8,128)} %first_in.3, ...), custom_call_target="tpu_custom_call" | custom-call | tf_op jit(solution)/shard_map/pallas_call | solution.py:481
  116.0 5.8 %shard_map.95 = (f32[64,4,1024]{2,1,0:T(4,128)}, f32[1,256,1024]{2,1,0:T(8,128)}, f32[1,256,1024]{2,1,0:T(8,128)}) custom-call(s32[64]{0:T(128)} %owner.3, f32[8,128]{1,0:T(8,128)} %get-tuple-element.6.graft, f32[64,4,1024]{2,1,0:T(4,128)} %get-tuple-element.7.received, f32[1,256,1024]{2,1,0:T(8,128)} %get-tuple-element.8.rot_in, f32[1,256,1024]{2,1,0:T(8,128)} %first_in.3, ...), custom_call_target="tpu_custom_call" | custom-call | tf_op jit(solution)/shard_map/pallas_call | solution.py:508
where the time goes:
time: 122 us
  Pallas kernels  121 us (99%)
  between operations  1.28 us (1%)
    pallas_call x1, Pallas kernels, body(): pl.pallas_call(kernel, out_shape=(jax.ShapeDtypeStruct((64, 4, 1024), F32...  115 us
    pallas_call x1, Pallas kernels, body(): pl.pallas_call(finish, out_shape=(jax.ShapeDtypeStruct((64, 4, 1024), F32...  5.83 us

commit v1 on v0

--- a/solution.py
+++ b/solution.py
@@ -14,7 +14,7 @@
 F32 = jnp.float32
 BF16 = jnp.bfloat16
 NC = 4
-NG = 4
+NG = 2
 PER = NC // NG
 CUTS = ((0, 128), (128, 128), (256, 256), (512, 256), (768, 256))
 W = 1024 // NC
@@ -126,8 +126,6 @@
         def _():
             rcopy(src, dst, name, swap).start()
 
-    fetch(left_in.at[0], lf, "L")
-
     @pl.when(home)
     def _():
         rcopy(right_in.at[0], rf.at[q], "RX", across).start()
@@ -135,6 +133,10 @@
         pltpu.make_async_copy(right_in.at[0], rf.at[q], sem(rsem, "R")).start()
         for i in range(1, 8):
             pl.semaphore_signal(bar.at[0], inc=1, device_id=zpeer(i), device_id_type=MESH)
+
+    @pl.when(away)
+    def _():
+        rcopy(right_in.at[0], rf.at[x], "R", swap).start()
 
     time = jnp.full((8, 128), steps[0].astype(F32))
     row = lax.broadcasted_iota(jnp.int32, (8, 128), 0)
@@ -162,9 +164,12 @@
         pl.semaphore_wait(bar.at[2], 1)
 
     for g in range(NG):
+        part = pl.ds(g * (Q // NG), Q // NG)
+        fetch(left_in.at[0, part], lf.at[part], "L")
+
         @pl.loop(0, 64)
         def _(t):
-            yo, zo, co = (y + t // 16) % 4, (z + (t // 2) % 8) % 8, (c + t) % 2
+            yo, zo, co = (y + t // 16) % 4, (z + 3 * (t // 2)) % 8, (c + t) % 2
             o = (yo * 8 + zo) * 2 + co
             xo = jnp.where(co == h, x, 3 - x)
             is_self = jnp.logical_and(home, t == 0)
@@ -178,11 +183,6 @@
             @pl.when(jnp.logical_not(is_self))
             def _():
                 rcopy(src, dst, "G", dev(xo, yo, zo, h), g).start()
-
-        @pl.when(away)
-        def _():
-            part = pl.ds(g * (Q // NG), Q // NG)
-            rcopy(right_in.at[0, part], rf.at[x, part], "R", swap).start()
 
     fetch(first_in.at[0], m1, "M1")
     fetch(second_in.at[0], m2, "M2")
@@ -206,19 +206,38 @@
             rh[k, rows, :] = high
             rl[k, rows, :] = low
 
+    @pl.when(away)
+    def _():
+        arrived(rf.at[q], "R")
+        rcopy(rf.at[q], rf.at[q], "RX", across).start()
+        rcopy(rf.at[q], rf.at[q], "RS", sib).start()
+
     @pl.when(home)
     def _():
         arrived(rf.at[q], "R")
         arrived(rf.at[q_xp], "RX")
         rcopy(rf.at[q_xp], rf.at[q_xp], "RF", sib).start()
+        arrived(rf.at[q_sib], "RS")
 
     @pl.when(away)
     def _():
         arrived(rf.at[q_sib], "RS")
         arrived(rf.at[q_xps], "RF")
 
-    split_right(2 * h)
-    split_right(2 * h + 1)
+    split_right(q)
+    split_right(q_sib)
+
+    @pl.when(away)
+    def _():
+        arrived(rf.at[q_xp], "RX")
+        rcopy(rf.at[q_xp], rf.at[q_xp], "RF", sib).start()
+
+    @pl.when(home)
+    def _():
+        arrived(rf.at[q_xps], "RF")
+
+    split_right(q_xp)
+    split_right(q_xps)
 
     arrived(lf, "L")
     for k in range(4):
@@ -256,13 +275,7 @@
         rcopy(c_snd.at[i], c_rcv.at[i], "C", sib, i).start()
         d_buf[i] = partial(q, i)
 
-    @pl.when(away)
-    def _():
-        arrived(rf.at[q], "R")
-        rcopy(rf.at[q], rf.at[q], "RX", across).start()
-        rcopy(rf.at[q], rf.at[q], "RS", sib).start()
-
-    def rotate(i):
+    for i in range(NC):
         arrived(c_rcv.at[i], "C", i)
         arrived(x_rcv.at[i], "X", i)
         k = (2 * h + i) % 4
@@ -272,31 +285,6 @@
             rot[...] = term
         else:
             rot[...] += term
-
-    @pl.when(away)
-    def _():
-        arrived(rf.at[q_xp], "RX")
-        rcopy(rf.at[q_xp], rf.at[q_xp], "RF", sib).start()
-
-    @pl.when(home)
-    def _():
-        arrived(rf.at[q_sib], "RS")
-        arrived(rf.at[q_xps], "RF")
-
-    split_right(2 - 2 * h)
-    split_right(3 - 2 * h)
-    for i in range(NC):
-        rotate(i)
-
-    fetch_out = rot_out.at[0]
-
-    @pl.when(home)
-    def _():
-        pltpu.make_async_copy(rot, fetch_out, sem(rsem, "RO")).start()
-
-    @pl.when(away)
-    def _():
-        rcopy(rot, fetch_out, "RO", swap).start()
 
     arrived(bias, "BI")
     arrived(m1, "M1")
@@ -354,7 +342,7 @@
 
         @pl.loop(0, 64)
         def _(t):
-            yo, zo, co = (y + t // 16) % 4, (z + (t // 2) % 8) % 8, (c + t) % 2
+            yo, zo, co = (y + t // 16) % 4, (z + 3 * (t // 2)) % 8, (c + t) % 2
             o = (yo * 8 + zo) * 2 + co
             is_self = jnp.logical_and(home, t == 0)
 
@@ -365,6 +353,10 @@
             @pl.when(jnp.logical_not(is_self))
             def _():
                 rcopy(back.at[o, :, cols], recv_o.at[slot, :, cols], "O", dev(q, yo, zo, co)).start()
+
+        if 1 <= j <= 2:
+            part = pl.ds((j - 1) * 128, 128)
+            fetch(rot.at[part], rot_out.at[0, part], "RO")
 
     arrived(sa_r, "SA")
     sb_v[...] = sa_v[...] + jnp.sum(sa_r[...], axis=0)
@@ -419,8 +411,9 @@
     owner, graft, received, rot_in, first_in, second_in, update, first_out, second_out,
     wire, rot, first, second, n1, n2, sin, sout,
 ):
-    parts = 2
+    parts = 4
     size = Q // parts
+    slots = 64 // parts
     copy = pltpu.make_async_copy
 
     def pieces(p):
@@ -437,19 +430,15 @@
             for k, (src, dst) in enumerate(((n1, first_out), (n2, second_out)))
         ]
 
-    incoming = copy(received, wire, sin.at[parts, 0])
-    incoming.start()
+    def incoming(p):
+        some = pl.ds(p * slots, slots)
+        return copy(received.at[some], wire.at[some], sin.at[p, 3])
+
     for p in range(parts):
         for piece in pieces(p):
             piece.start()
-    scale = graft[0:1, 0:1]
-    incoming.wait()
-
-    @pl.loop(0, 64)
-    def _(o):
-        wire[o] = wire[o] * scale
-        copy(wire.at[o], update.at[owner[o]], sout.at[parts, 0]).start()
-
+    for p in range(parts):
+        incoming(p).start()
     for p in range(parts):
         for piece in pieces(p):
             piece.wait()
@@ -459,6 +448,16 @@
         n2[rows, :] = BETA_TWO * second[rows, :] + (1.0 - BETA_TWO) * value * value
         for result in results(p):
             result.start()
+    scale = graft[0:1, 0:1]
+    for p in range(parts):
+        incoming(p).wait()
+
+        @pl.loop(0, slots, unroll=4)
+        def _(i):
+            o = p * slots + i
+            wire[o] = wire[o] * scale
+            copy(wire.at[o], update.at[owner[o]], sout.at[parts, 0]).start()
+
     for p in range(parts):
         for result in results(p):
             result.wait()
@@ -516,7 +515,7 @@
         out_specs=(anywhere, anywhere, anywhere),
         scratch_shapes=[
             wire, rows_f, rows_f, rows_f, rows_f, rows_f,
-            pltpu.SemaphoreType.DMA((3, 3)), pltpu.SemaphoreType.DMA((3, 3)),
+            pltpu.SemaphoreType.DMA((4, 4)), pltpu.SemaphoreType.DMA((5, 2)),
         ],
         compiler_params=pltpu.CompilerParams(vmem_limit_bytes=56 * 1024 * 1024),
     )(owner_table, graft, received, rotated, first_moment, second_moment)

time: 122 us -> 121 us (level)
  Pallas kernels: 121 us -> 119 us
    pallas_call x1, Pallas kernels: 5.83 us -> 3.97 us  [body(): pl.pallas_call(finish, out_shape=(jax.ShapeDtypeStruct((64, 4, 1024), F32...]
where the time goes in v1:
time: 121 us
  Pallas kernels  119 us (98%)
  between operations  1.28 us (1%)
    pallas_call x1, Pallas kernels, body(): pl.pallas_call(kernel, out_shape=(jax.ShapeDtypeStruct((64, 4, 1024), F32...  115 us
    pallas_call x1, Pallas kernels, body(): pl.pallas_call(finish, out_shape=(jax.ShapeDtypeStruct((64, 4, 1024), F32...  3.97 us

profile of v1, /device:TPU:1, one launch (start us, length us, event | category | flops | bytes accessed | tf_op | source)
XLA Modules:
  0.0 120.6 jit_solution(5714427013788030209)
XLA Ops:
  1.3 115.3 %shard_map.94 = (f32[64,4,1024]{2,1,0:T(4,128)}, f32[1,256,1024]{2,1,0:T(8,128)}, f32[8,128]{1,0:T(8,128)}) custom-call(s32[64]{0:T(128)} %owner.3, s32[1]{0:T(128)S(6)} %copy.10.steps, f32[64,4,1024]{2,1,0:T(4,128)} %grad_in.1, f32[1,256,1024]{2,1,0:T(8,128)} %left_in.1, f32[1,256,1024]{2,1,0:T(8,128)} %right_in.1, f32[1,256,1024]{2,1,0:T(8,128)} %first_in.3, ...), custom_call_target="tpu_custom_call" | custom-call | tf_op jit(solution)/shard_map/pallas_call | solution.py:480
  116.6 4.0 %shard_map.95 = (f32[64,4,1024]{2,1,0:T(4,128)}, f32[1,256,1024]{2,1,0:T(8,128)}, f32[1,256,1024]{2,1,0:T(8,128)}) custom-call(s32[64]{0:T(128)} %owner.3, f32[8,128]{1,0:T(8,128)} %get-tuple-element.6.graft, f32[64,4,1024]{2,1,0:T(4,128)} %get-tuple-element.7.received, f32[1,256,1024]{2,1,0:T(8,128)} %get-tuple-element.8.rot_in, f32[1,256,1024]{2,1,0:T(8,128)} %first_in.3, ...), custom_call_target="tpu_custom_call" | custom-call | tf_op jit(solution)/shard_map/pallas_call | solution.py:507

commit v2 on v1

--- a/solution.py
+++ b/solution.py
@@ -104,14 +104,14 @@
         return dev(xc // 2, y, z, xc % 2)
 
     gate = pltpu.get_barrier_semaphore()
-    for i in range(1, 8):
-        pl.semaphore_signal(gate, inc=1, device_id=xcpeer(i), device_id_type=MESH)
-
     @pl.when(home)
     def _():
         for count, peer in ((8, zpeer), (4, ypeer)):
             for i in range(1, count):
                 pl.semaphore_signal(gate, inc=1, device_id=peer(i), device_id_type=MESH)
+
+    for i in range(1, 8):
+        pl.semaphore_signal(gate, inc=1, device_id=xcpeer(i), device_id_type=MESH)
 
     grad_copy = pltpu.make_async_copy(grad_in, grad, sem(rsem, "GI"))
     grad_copy.start()

time: 121 us -> 121 us (level)
  no operation moved by 1% of the time
where the time goes in v2:
time: 121 us
  Pallas kernels  120 us (99%)
  between operations  1.28 us (1%)
    pallas_call x1, Pallas kernels, body(): pl.pallas_call(kernel, out_shape=(jax.ShapeDtypeStruct((64, 4, 1024), F32...  116 us
    pallas_call x1, Pallas kernels, body(): pl.pallas_call(finish, out_shape=(jax.ShapeDtypeStruct((64, 4, 1024), F32...  3.97 us

profile of v2, /device:TPU:1, one launch (start us, length us, event | category | flops | bytes accessed | tf_op | source)
XLA Modules:
  0.0 120.8 jit_solution(18325969100725931982)
XLA Ops:
  1.3 115.5 %shard_map.94 = (f32[64,4,1024]{2,1,0:T(4,128)}, f32[1,256,1024]{2,1,0:T(8,128)}, f32[8,128]{1,0:T(8,128)}) custom-call(s32[64]{0:T(128)} %owner.3, s32[1]{0:T(128)S(6)} %copy.10.steps, f32[64,4,1024]{2,1,0:T(4,128)} %grad_in.1, f32[1,256,1024]{2,1,0:T(8,128)} %left_in.1, f32[1,256,1024]{2,1,0:T(8,128)} %right_in.1, f32[1,256,1024]{2,1,0:T(8,128)} %first_in.3, ...), custom_call_target="tpu_custom_call" | custom-call | tf_op jit(solution)/shard_map/pallas_call | solution.py:480
  116.8 4.0 %shard_map.95 = (f32[64,4,1024]{2,1,0:T(4,128)}, f32[1,256,1024]{2,1,0:T(8,128)}, f32[1,256,1024]{2,1,0:T(8,128)}) custom-call(s32[64]{0:T(128)} %owner.3, f32[8,128]{1,0:T(8,128)} %get-tuple-element.6.graft, f32[64,4,1024]{2,1,0:T(4,128)} %get-tuple-element.7.received, f32[1,256,1024]{2,1,0:T(8,128)} %get-tuple-element.8.rot_in, f32[1,256,1024]{2,1,0:T(8,128)} %first_in.3, ...), custom_call_target="tpu_custom_call" | custom-call | tf_op jit(solution)/shard_map/pallas_call | solution.py:507
